TPU v7x, 32 devices: a whole 2x2x4 slice. The times are simulated.
32 devices in a mesh: group: 2 (over x), link: 16 (over z, y, core).
Axes of the slice: x: 2, y: 2, z: 4, core: 2. Of those that a mesh axis runs over, the one named last changes fastest.
Arguments:
- ray_rows: float32 [16384, 128], P(('group', 'link')), parts along dimension 0, may hold values from -6 to 6
- visible: int32 [256, 256], P(('group', 'link')), parts along dimension 0, may hold values from 0 to 8191, as said below
- base_tap: int32 [256, 256], P(('group', 'link')), parts along dimension 0, may hold values from 0 to 63
- frac_index: int32 [256, 256], P(('group', 'link')), parts along dimension 0, may hold values from 0 to 15
- elem_tap: int32 [8, 2048], P(None, 'link'), may hold values from 0 to 1073741823
- elem_gain: float32 [8, 2048], P(None, 'link'), may hold values from -0.375 to 0.375
Outputs:
- received: float32 [256, 2048, 128], P(('group', 'link')), parts along dimension 0
There are 2 independent parts, one for each index of `group`. A program takes and returns all parts, laid end to end along the dimension named above; an argument that names none is the same for every part. Nothing has to cross between parts.
Inputs may be any that keep to these rules, and one draw needn't show every extreme that they name: `visible`: scatterer s is owned by link device s // 512. Among the 2048 entries of the UEs of one device (aligned blocks of 8 rows), at most 256 name scatterers of any one owner, and some owner is named exactly 256 times in every block. An id may repeat. Scatterer ids and other integer indices may be sent packed several to a 32-bit word; this is the one exception to the rule of bits below.
All inputs are finite; a program needn't handle non-finite values.
Results may differ from a plain program's by a relative error of at most 0.000073.
Values sent between devices are 32-bit elements; how exact they have to be, the bound alone decides.
A program may use at most 512 MiB of HBM per device.

v0:
```python
import jax
import jax.numpy as jnp
from jax import lax
from jax.sharding import PartitionSpec as P

SAMPLES = 128
TAP_SPAN = 32
BASE_SPAN = 64
FRACS = 16
CLUSTERS = 8


def lagrange(frac_flat):
    mu_val = frac_flat.astype(jnp.float32) / FRACS
    first = -mu_val * (mu_val - 1.0) * (mu_val - 2.0) / 6.0
    second = (mu_val + 1.0) * (mu_val - 1.0) * (mu_val - 2.0) / 2.0
    third = -(mu_val + 1.0) * mu_val * (mu_val - 2.0) / 2.0
    fourth = (mu_val + 1.0) * mu_val * (mu_val - 1.0) / 6.0
    return jnp.stack([first, second, third, fourth], axis=1)


def farrow_filter(picked, frac_flat):
    coeffs = lagrange(frac_flat)
    length = picked.shape[1]
    padded = jnp.pad(picked, ((0, 0), (3, 3)))
    filtered = jnp.zeros((picked.shape[0], length + 3), jnp.float32)
    for shift_k in range(4):
        filtered = (
            filtered
            + coeffs[:, shift_k : shift_k + 1] * padded[:, 3 - shift_k : 3 - shift_k + length + 3]
        )
    return filtered


def skew_sum(stacked, width):
    lead = stacked.shape[:-2]
    span = stacked.shape[-2]
    length = stacked.shape[-1]
    padded = jnp.pad(stacked, [(0, 0)] * len(lead) + [(0, 0), (0, span)])
    total_len = length + span
    flat = padded.reshape(lead + (span * total_len,))[..., : span * (total_len - 1)]
    sheared = flat.reshape(lead + (span, total_len - 1))
    return jnp.sum(sheared, axis=-2)[..., :width]


def element_sum(zones, elem_tap, elem_gain):
    reduced_tap = elem_tap % TAP_SPAN
    windows = jnp.stack(
        [zones[:, :, TAP_SPAN - delay : TAP_SPAN - delay + SAMPLES] for delay in range(TAP_SPAN)],
        axis=2,
    )
    select = (reduced_tap[:, None, :] == jnp.arange(TAP_SPAN)[None, :, None]).astype(jnp.float32)
    table = select * elem_gain[:, None, :]
    return jnp.einsum("ucdn,cde->uen", windows, table, precision=lax.Precision.HIGHEST)


def on_device(ray_rows, visible, base_tap, frac_index, elem_tap, elem_gain):
    taps_all, gains_all = (
        lax.all_gather(elem_tap, "link", axis=1, tiled=True),
        lax.all_gather(elem_gain, "link", axis=1, tiled=True),
    )
    flat_ids = visible.reshape(-1)
    entries = flat_ids.shape[0]
    local_count = ray_rows.shape[0]
    owners_count = lax.axis_size("link")
    capacity = 2 * entries // owners_count
    width = SAMPLES + TAP_SPAN
    owner_id = flat_ids // local_count
    member = (owner_id[:, None] == jnp.arange(owners_count)[None, :]).astype(jnp.int32)
    slot_id = jnp.sum(member * (jnp.cumsum(member, axis=0) - 1), axis=1)
    owner_hot = member.astype(jnp.float32)
    slot_hot = (slot_id[:, None] == jnp.arange(capacity)[None, :]).astype(jnp.float32)
    local_id = (flat_ids % local_count).astype(jnp.float32)
    requests = jnp.einsum(
        "eo,es->os", owner_hot, slot_hot * local_id[:, None], precision=lax.Precision.HIGHEST
    ).astype(jnp.int32)
    fetched = ray_rows[lax.all_to_all(requests, "link", split_axis=0, concat_axis=0, tiled=True)]
    arrived = lax.all_to_all(fetched, "link", split_axis=0, concat_axis=0, tiled=True)
    picked = arrived.reshape(owners_count * capacity, -1)[owner_id * capacity + slot_id]
    filtered = farrow_filter(picked, frac_index.reshape(-1))
    users_here = visible.shape[0]
    code = visible % CLUSTERS * BASE_SPAN + base_tap
    onehot = (code[:, :, None] == jnp.arange(CLUSTERS * BASE_SPAN)[None, None, :]).astype(
        jnp.float32
    )
    stacked = jnp.einsum(
        "uvg,uvj->ugj",
        onehot,
        filtered.reshape(users_here, visible.shape[1], -1),
        precision=lax.Precision.HIGHEST,
    )
    zones = skew_sum(stacked.reshape(users_here, CLUSTERS, BASE_SPAN, -1), width)
    return element_sum(zones, taps_all, gains_all)


def solution(mesh):
    in_specs = (
        P(("group", "link"), None),
        P(("group", "link"), None),
        P(("group", "link"), None),
        P(("group", "link"), None),
        P(None, "link"),
        P(None, "link"),
    )
    out_specs = P(("group", "link"), None, None)
    return jax.shard_map(
        on_device, mesh=mesh, in_specs=in_specs, out_specs=out_specs, check_vma=False
    )
```

profile of v0, /device:TPU:0, one launch (start us, length us, event | category | flops | bytes accessed | tf_op | source)
XLA Modules:
  0.0 161.4 jit_solution(18223277849417504579)
XLA Ops:
  0.0 0.0 copy-start
  0.0 0.7 reshape.235
  0.7 0.7 copy.115
  1.5 4.5 %reduce-window.6 = s32[16,16,128]{2,1,0:T(8,128)S(1)} reduce-window(s32[16,16,128]{2,1,0:T(8,128)S(1)} %fusion.29, s32[]{:T(128)} %constant.74.clone.1), window={size=1x1x128 pad=0_0x0_0x127_0}, to_apply=%region_0.1 | reduce-window | flops 4161536 | bytes 262148 | tf_op jit(solution)/shard_map/reduce-window
  6.0 0.4 slice_reduce_fusion
  6.5 0.2 reduce-window.9
  6.6 0.1 add_add_fusion
  6.8 0.1 fusion.26
  6.8 1.3 fusion.16
  8.1 13.7 %all_to_all.17 = s32[16,1,256]{2,1,0:T(1,128)S(1)} all-to-all(s32[16,1,256]{2,1,0:T(1,128)S(1)} %copy.73), channel_id=1, replica_groups=mesh['group'=2,'link'=16] {'link'}, dimensions={0} | all-to-all | bytes 32768 | tf_op jit(solution)/shard_map/all_to_all | solution.py:77
  21.9 0.0 copy-done
  21.9 14.2 %gather_fusion = f32[4096,128]{1,0:T(8,128)} fusion(f32[512,128]{1,0:T(8,128)S(1)} %copy-done, s32[4096]{0:T(1024)S(1)} %broadcast_clamp_fusion), kind=kCustom, calls=%fused_computation | custom fusion | bytes 4210688 | tf_op jit(solution)/shard_map/gather | solution.py:77
  36.1 0.0 copy-start.4
  36.1 0.0 copy-start.1
  36.1 0.0 copy-start.5
  36.1 0.0 copy-start.6
  36.1 0.0 copy-start.3
  36.1 3.9 %all-to-all-start.1 = ((f32[16,256,128]{2,1,0:T(8,128)}), f32[16,256,128]{2,1,0:T(8,128)S(1)}, u32[]{:S(2)}, u32[]{:S(2)}) async-start(f32[16,256,128]{2,1,0:T(8,128)} %bitcast.143), calls=%async_computation.1 | async-start | bytes 4194304 | tf_op jit(solution)/shard_map/all_to_all | solution.py:78
  40.0 0.0 copy-done.4
  40.0 0.0 copy-done.1
  40.0 0.0 copy-done.5
  40.0 50.6 %all_gather.6 = s32[8,2048]{1,0:T(8,128)S(1)} all-gather(s32[8,128]{1,0:T(8,128)S(1)} %copy-done.5), channel_id=1, replica_groups=mesh['group'=2,'link'=16] {'link'}, dimensions={1}, use_global_device_ids=true | all-gather | bytes 69632 | tf_op jit(solution)/shard_map/all_gather | solution.py:59
  90.7 0.0 copy-done.6
  90.7 27.0 %all_gather.7 = f32[8,2048]{1,0:T(8,128)S(1)} all-gather(f32[8,128]{1,0:T(8,128)S(1)} %copy-done.6), channel_id=1, replica_groups=mesh['group'=2,'link'=16] {'link'}, dimensions={1}, use_global_device_ids=true | all-gather | bytes 69632 | tf_op jit(solution)/shard_map/all_gather | solution.py:60
  117.7 0.1 compare_select_fusion.1
  117.7 0.0 copy-done.3
  117.8 0.6 add_select_fusion
  118.4 0.0 all-to-all-done.1
  118.4 5.5 %gather_fusion.1 = f32[2048,128]{1,0:T(8,128)S(1)} fusion(f32[4096,128]{1,0:T(8,128)S(1)} %bitcast.140, s32[2048]{0:T(1024)S(1)} %broadcast_clamp_fusion.1), kind=kCustom, calls=%fused_computation.1 | custom fusion | bytes 2105344 | tf_op jit(solution)/shard_map/gather | solution.py:79
  123.9 3.0 %fusion.4 = f32[2048,131]{1,0:T(8,128)S(1)} fusion(f32[2048,128]{1,0:T(8,128)S(1)} %gather_fusion.1, f32[2048]{0:T(1024)S(1)} %get-tuple-element.39, f32[2048]{0:T(1024)S(1)} %get-tuple-element.40, f32[2048]{0:T(1024)S(1)} %get-tuple-element.38, f32[2048]{0:T(1024)S(1)} %get-tuple-element.37), kind=kLoop, calls=%fused_computation.12 | loop fusion | flops 1878016 | bytes 2154496 | tf_op jit(solution)/shard_map/add | solution.py:29
  126.9 3.9 %fusion = f32[8,512,131]{2,1,0:T(8,128)S(1)} fusion(f32[8,256,131]{2,1,0:T(8,128)S(1)} %bitcast.142, s32[8,256]{1,0:T(8,128)S(1)} %fusion.41), kind=kOutput, calls=%fused_computation.4 | convolution fusion | flops 1649410048 | bytes 3227648
  130.8 2.3 %pad.9.clone = f32[8,8,64,195]{3,2,1,0:T(8,128)} pad(f32[8,8,64,131]{3,2,1,0:T(8,128)S(1)} %bitcast.141, f32[]{:T(128)} %constant.77.clone.1), padding=0_0x0_0x0_0x0_64 | pad | bytes 5341188 | tf_op jit(solution)/shard_map/jit(_pad)/pad | solution.py:39
  133.2 4.0 %reshape.241 = f32[8,8,12480]{2,1,0:T(8,128)S(1)} reshape(f32[8,8,64,195]{3,2,1,0:T(8,128)} %pad.9.clone) | data formatting | bytes 6389760 | tf_op jit(solution)/shard_map/reshape | solution.py:41
  137.2 1.9 %slice.195 = f32[8,8,12416]{2,1,0:T(8,128)} slice(f32[8,8,12480]{2,1,0:T(8,128)S(1)} %reshape.241), slice={[0:8], [0:8], [0:12416]} | slice | bytes 6356992 | tf_op jit(solution)/shard_map/slice | solution.py:41
  139.0 8.2 %reshape.242 = f32[8,8,64,194]{3,2,1,0:T(8,128)} reshape(f32[8,8,12416]{2,1,0:T(8,128)} %slice.195) | data formatting | bytes 6356992 | tf_op jit(solution)/shard_map/reshape | solution.py:42
  147.2 2.8 %reduce_sum.22 = f32[8,8,194]{2,1,0:T(8,128)S(1)} reduce(f32[8,8,64,194]{3,2,1,0:T(8,128)} %reshape.242, f32[]{:T(128)} %constant.77.clone.1), dimensions={2}, to_apply=%region_3.4 | reduce | flops 782208 | bytes 3228164 | tf_op jit(solution)/shard_map/reduce_sum | solution.py:43
  150.0 0.0 copy-start.2
  150.0 0.2 fusion.50
  150.2 0.2 fusion.49
  150.4 1.6 stack.135
  152.0 0.0 copy-done.2
  152.0 9.3 %convolution_bitcast_fusion = f32[8,2048,128]{2,1,0:T(8,128)} fusion(f32[8,8,32,128]{3,2,1,0:T(8,128)S(1)} %stack.135, f32[8,2048]{1,0:T(8,128)S(1)} %all_gather.7, s32[8,2048]{1,0:T(8,128)S(1)} %copy-done.2), kind=kOutput, calls=%fused_computation.2 | convolution fusion | flops 6443499520 | bytes 9568256 | tf_op jit(solution)/shard_map/ucdn,cde->uen/dot_general | solution.py:54
  (12 shorter events, 0.1 us)
Async XLA Ops:
  0.0 21.9 %copy-start = (f32[512,128]{1,0:T(8,128)S(1)}, f32[512,128]{1,0:T(8,128)}, u32[]{:S(2)}) copy-start(f32[512,128]{1,0:T(8,128)} %param.6) | copy-start | bytes 786436
  36.1 3.9 %copy-start.4 = (s32[8,256]{1,0:T(8,128)S(1)}, s32[8,256]{1,0:T(8,128)}, u32[]{:S(2)}) copy-start(s32[8,256]{1,0:T(8,128)} %param.9) | copy-start | bytes 24580
  36.1 3.9 %copy-start.1 = (s32[8,256]{1,0:T(8,128)S(1)}, s32[8,256]{1,0:T(8,128)}, u32[]{:S(2)}) copy-start(s32[8,256]{1,0:T(8,128)} %param.7) | copy-start | bytes 24580
  36.1 4.0 %copy-start.5 = (s32[8,128]{1,0:T(8,128)S(1)}, s32[8,128]{1,0:T(8,128)}, u32[]{:S(2)}) copy-start(s32[8,128]{1,0:T(8,128)} %param.10) | copy-start | bytes 12292
  36.1 54.6 %copy-start.6 = (f32[8,128]{1,0:T(8,128)S(1)}, f32[8,128]{1,0:T(8,128)}, u32[]{:S(2)}) copy-start(f32[8,128]{1,0:T(8,128)} %param.11) | copy-start | bytes 12292
  36.1 81.6 %copy-start.3 = (s32[8,256]{1,0:T(8,128)S(1)}, s32[8,256]{1,0:T(8,128)}, u32[]{:S(2)}) copy-start(s32[8,256]{1,0:T(8,128)} %param.8) | copy-start | bytes 24580
  36.1 82.3 %all-to-all-start.1 = ((f32[16,256,128]{2,1,0:T(8,128)}), f32[16,256,128]{2,1,0:T(8,128)S(1)}, u32[]{:S(2)}, u32[]{:S(2)}) async-start(f32[16,256,128]{2,1,0:T(8,128)} %bitcast.143), calls=%async_computation.1 | async-start | bytes 4194304 | tf_op jit(solution)/shard_map/all_to_all | solution.py:78
  150.0 2.0 %copy-start.2 = (s32[8,2048]{1,0:T(8,128)S(1)}, s32[8,2048]{1,0:T(8,128)}, u32[]{:S(2)}) copy-start(s32[8,2048]{1,0:T(8,128)} %add_select_fusion) | copy-start | bytes 196612
where the time goes:
time: 162 us; the launch traced here: 161 us
  blocking collectives  91.3 us (56%)
  local copies, waits for them, and re-layouts  40 us (25%)
  matrix products  14.5 us (9%)
  other arithmetic  11.5 us (7%)
  starting transfers between devices  3.86 us (2%)
    all_gather x1, blocking collectives, on_device(): lax.all_gather(elem_tap, 'link', axis=1, tiled=True)  50.6 us
    all_gather x1, blocking collectives, on_device(): lax.all_gather(elem_gain, 'link', axis=1, tiled=True)  27 us
    gather x1, local copies, waits for them, and re-layouts, on_device(): ray_rows[lax.all_to_all(requests, 'link', split_axis=0, concat_axis=0, ti...  14.2 us
    all_to_all x1, blocking collectives, on_device(): lax.all_to_all(requests, 'link', split_axis=0, concat_axis=0, tiled=True)  13.7 us
    dot_general x1, matrix products, element_sum(): jnp.einsum('ucdn,cde->uen', windows, table, precision=lax.Precision.HIGHEST)  9.35 us
    reshape x1, local copies, waits for them, and re-layouts, skew_sum(): sheared = flat.reshape(lead + (span, total_len - 1))  8.19 us
    gather x1, local copies, waits for them, and re-layouts, on_device(): arrived.reshape(owners_count * capacity, -1)[owner_id * capacity + slot_id]  5.46 us
    another operation x2, other arithmetic  4.71 us
  transfers between devices with their start and end apart: 1, of which 0 were waited for; matrix products, arithmetic and copies ran while one was open for 0% of the time, Pallas kernels for 0%

commit v1 on v0

v1 whole, which is shorter than its diff:
```python
import functools

import jax
import jax.numpy as jnp
from jax import lax
from jax.experimental import pallas as pl
from jax.experimental.pallas import tpu as pltpu
from jax.sharding import PartitionSpec as P

SAMPLES = 128
TAP_SPAN = 32
BASE_SPAN = 64
FRACS = 16
CLUSTERS = 8
LANES = 128
TAPS = 4
PLACE_ROWS = -(-(BASE_SPAN + TAPS - 1) * CLUSTERS // 16) * 16
SETS = 2

F32 = jnp.float32
BF16 = jnp.bfloat16


def flip(value, mask):
    result = value
    bit = 1
    while bit <= mask:
        if mask & bit:
            result = result + bit * (1 - 2 * ((value // bit) % 2))
        bit *= 2
    return result


def split(value):
    high = value.astype(BF16)
    return high, (value - high.astype(F32)).astype(BF16)


def zone_kernel(
    n, sets,
    ray_ref, vis_ref, base_ref, frac_ref, tap_ref, gain_ref,
    zone_ref, elem_ref,
    rays, elem_all, meta_own, meta_all, id_cols, ray_split, picked, zone_part, zone_got,
    ray_send, ray_recv, fwd_send, fwd_recv, meta_send, meta_recv, elem_send, elem_recv,
    zone_send, zone_recv,
):
    per_set = n // sets
    chips = per_set // 2
    me = lax.axis_index("link")
    own_set = me // per_set
    place = me % per_set
    chip = place // 2
    core = place % 2
    sibling = me + 1 - 2 * core
    users, slots = vis_ref.shape
    owned = ray_ref.shape[0]

    barrier = pltpu.get_barrier_semaphore()
    for step in range(1, n):
        pl.semaphore_signal(
            barrier, inc=1, device_id={"link": (me + step) % n}, device_id_type=pl.DeviceIdType.MESH
        )
    words = vis_ref[...] * (BASE_SPAN * FRACS) + base_ref[...] * FRACS + frac_ref[...]
    for part in range(slots // LANES):
        meta_own[part] = words[:, part * LANES : (part + 1) * LANES]
    meta_all[0] = meta_own[...]
    elem_all[me, 0:CLUSTERS] = gain_ref[...]
    elem_all[me, CLUSTERS : 2 * CLUSTERS] = (tap_ref[...] & (TAP_SPAN - 1)).astype(F32)
    pl.semaphore_wait(barrier, n - 1)

    def remote(src, dst, send, recv, target):
        return pltpu.make_async_remote_copy(
            src_ref=src, dst_ref=dst, send_sem=send, recv_sem=recv,
            device_id={"link": target}, device_id_type=pl.DeviceIdType.MESH,
        )

    metas = [
        remote(meta_own, meta_all.at[q], meta_send.at[q], meta_recv.at[q],
               flip(own_set, q) * per_set + place)
        for q in range(1, sets)
    ]
    for copy in metas:
        copy.start()
    own_copy = remote(ray_ref, rays.at[1], fwd_send.at[0], fwd_recv.at[0], sibling)
    own_copy.start()
    far = [
        remote(ray_ref, rays.at[2 * k], ray_send.at[k], ray_recv.at[k],
               own_set * per_set + flip(chip, k) * 2 + core)
        for k in range(1, chips)
    ]
    for copy in far:
        copy.start()
    elems = [
        remote(elem_all.at[me], elem_all.at[me], elem_send.at[step], elem_recv.at[step],
               (me + step) % n)
        for step in range(1, n)
    ]
    for copy in elems:
        copy.start()

    def expand(q):
        def body(user, carry):
            for part in range(slots // LANES):
                row = meta_all[q, part, pl.ds(user, 1), :]
                ids = lax.shift_right_logical(row, jnp.int32(10))
                square = jnp.transpose(jnp.broadcast_to(ids, (LANES, LANES)))
                at = pl.multiple_of((q * users + user) * slots + part * LANES, LANES)
                id_cols[pl.ds(at, LANES), :] = square
            return carry

        lax.fori_loop(0, users, body, 0)

    def prepare(k):
        for other in range(2):
            block = ray_ref[...] if k == 0 and other == 0 else rays[2 * k + other]
            high, low = split(block)
            ray_split[other * owned : (other + 1) * owned, 0:LANES] = high
            ray_split[other * owned : (other + 1) * owned, LANES : 2 * LANES] = low

    def pick(k, first_chunk, last_chunk):
        first = own_set * per_set + flip(chip, k) * 2
        bases = ((first + core) * owned, (first + 1 - core) * owned)

        def body(chunk, carry):
            at = pl.multiple_of(chunk * slots, slots)
            ids = id_cols[pl.ds(at, slots), :]
            lane = lax.broadcasted_iota(jnp.int32, (slots, LANES), 1)
            hot = []
            for start in bases:
                shifted = ids - (lane + start)
                for tile in range(owned // LANES):
                    hot.append(jnp.where(shifted == tile * LANES, F32(1), F32(0)).astype(BF16))
            found = jnp.dot(
                jnp.concatenate(hot, axis=1), ray_split[...], preferred_element_type=F32
            )
            if k == 0:
                picked[pl.ds(at, slots), :] = found
            else:
                picked[pl.ds(at, slots), :] += found
            return carry

        lax.fori_loop(first_chunk, last_chunk, body, 0)

    expand(0)
    own_copy.wait()
    prepare(0)
    pick(0, 0, users)
    for q in range(1, sets):
        metas[q - 1].wait()
        expand(q)
    if sets > 1:
        pick(0, users, sets * users)
    forwards = []
    for k in range(1, chips):
        far[k - 1].wait_recv()
        copy = remote(rays.at[2 * k], rays.at[2 * k + 1], fwd_send.at[k], fwd_recv.at[k], sibling)
        copy.start()
        forwards.append(copy)
        copy.wait_recv()
        prepare(k)
        pick(k, 0, sets * users)

    def zones_of(q):
        def body(user, carry):
            row = jnp.concatenate(
                [meta_all[q, part, pl.ds(user, 1), :] for part in range(slots // LANES)], axis=1
            )
            frac = (row & (FRACS - 1)).astype(F32) * F32(1.0 / FRACS)
            base = lax.shift_right_logical(row, jnp.int32(4)) & (BASE_SPAN - 1)
            cluster = lax.shift_right_logical(row, jnp.int32(10)) & (CLUSTERS - 1)
            weights = (
                -frac * (frac - 1.0) * (frac - 2.0) / 6.0,
                (frac + 1.0) * (frac - 1.0) * (frac - 2.0) / 2.0,
                -(frac + 1.0) * frac * (frac - 2.0) / 2.0,
                (frac + 1.0) * frac * (frac - 1.0) / 6.0,
            )
            offset = lax.broadcasted_iota(jnp.int32, (PLACE_ROWS, slots), 0) - (
                base * CLUSTERS + cluster
            )
            matrix = jnp.zeros((PLACE_ROWS, slots), F32)
            for tap in range(TAPS):
                matrix = jnp.where(offset == tap * CLUSTERS, weights[tap], matrix)
            high, low = split(matrix)
            at = pl.multiple_of((q * users + user) * slots, slots)
            rows = picked[pl.ds(at, slots), :].astype(BF16)
            main = jnp.dot(high, rows, preferred_element_type=F32)
            rest = jnp.dot(low, rows[:, 0:LANES], preferred_element_type=F32)
            stacked = main[:, 0:LANES] + main[:, LANES : 2 * LANES] + rest
            lane = lax.broadcasted_iota(jnp.int32, (CLUSTERS, LANES), 1)
            early = stacked[0:CLUSTERS]
            late = jnp.zeros((CLUSTERS, LANES), F32)
            for delay in range(1, BASE_SPAN + TAPS - 1):
                turned = pltpu.roll(
                    stacked[delay * CLUSTERS : (delay + 1) * CLUSTERS], delay, axis=1
                )
                early = early + jnp.where(lane >= delay, turned, F32(0))
                late = late + jnp.where(lane < delay, turned, F32(0))
            out = pl.multiple_of(user * CLUSTERS, CLUSTERS)
            zone_part[q, pl.ds(out, CLUSTERS), 0:LANES] = early
            zone_part[q, pl.ds(out, CLUSTERS), LANES : 2 * LANES] = late
            return carry

        lax.fori_loop(0, users, body, 0)

    backs = []
    for q in range(1, sets):
        zones_of(q)
        copy = remote(zone_part.at[q], zone_got.at[q], zone_send.at[q], zone_recv.at[q],
                      flip(own_set, q) * per_set + place)
        copy.start()
        backs.append(copy)
    zones_of(0)
    for copy in elems:
        copy.wait_recv()
    elem_ref[...] = jnp.concatenate([elem_all[owner] for owner in range(n)], axis=1)
    total = zone_part[0]
    for q in range(1, sets):
        backs[q - 1].wait()
        total = total + zone_got[q]
    zone_ref[...] = total
    for copy in elems:
        copy.wait_send()
    for copy in far:
        copy.wait_send()
    for copy in forwards:
        copy.wait_send()


def element_kernel(zone_ref, elem_ref, out_ref, windows):
    users = zone_ref.shape[0] // CLUSTERS
    depth = TAP_SPAN * CLUSTERS

    @pl.when(pl.program_id(0) == 0)
    def _():
        lane = lax.broadcasted_iota(jnp.int32, (CLUSTERS, LANES), 1)
        for user in range(users):
            early = zone_ref[user * CLUSTERS : (user + 1) * CLUSTERS, 0:LANES]
            late = zone_ref[user * CLUSTERS : (user + 1) * CLUSTERS, LANES : 2 * LANES]
            tiles = []
            for delay in range(TAP_SPAN):
                ahead = TAP_SPAN - delay
                tiles.append(pltpu.roll(jnp.where(lane >= ahead, early, late), LANES - ahead, axis=1))
            high, low = split(jnp.concatenate(tiles, axis=0))
            at = user * LANES
            windows[0:depth, at : at + LANES] = high
            windows[depth : 2 * depth, at : at + LANES] = high
            windows[2 * depth : 3 * depth, at : at + LANES] = low

    gain = elem_ref[0:CLUSTERS]
    tap = elem_ref[CLUSTERS : 2 * CLUSTERS]
    table = jnp.concatenate(
        [jnp.where(tap == F32(delay), gain, F32(0)) for delay in range(TAP_SPAN)], axis=0
    )
    high, low = split(jnp.transpose(table))
    result = jnp.dot(
        jnp.concatenate([high, low, high], axis=1), windows[...], preferred_element_type=F32
    )
    for user in range(users):
        out_ref[user] = result[:, user * LANES : (user + 1) * LANES]


def on_device(n, ray_rows, visible, base_tap, frac_index, elem_tap, elem_gain):
    users, slots = visible.shape
    owned = ray_rows.shape[0]
    per_dev = elem_tap.shape[1]
    elements = n * per_dev
    sets = SETS
    per_set = n // sets
    chips = per_set // 2
    dma = pltpu.SemaphoreType.DMA
    vmem = pl.BlockSpec(memory_space=pltpu.VMEM)
    zones, elem = pl.pallas_call(
        functools.partial(zone_kernel, n, sets),
        out_shape=(
            jax.ShapeDtypeStruct((users * CLUSTERS, 2 * LANES), F32),
            jax.ShapeDtypeStruct((2 * CLUSTERS, elements), F32),
        ),
        in_specs=[vmem] * 6,
        out_specs=(vmem, vmem),
        scratch_shapes=[
            pltpu.VMEM((per_set, owned, LANES), F32),
            pltpu.VMEM((n, 2 * CLUSTERS, per_dev), F32),
            pltpu.VMEM((slots // LANES, users, LANES), jnp.int32),
            pltpu.VMEM((sets, slots // LANES, users, LANES), jnp.int32),
            pltpu.VMEM((sets * users * slots, LANES), jnp.int32),
            pltpu.VMEM((2 * owned, 2 * LANES), BF16),
            pltpu.VMEM((sets * users * slots, 2 * LANES), F32),
            pltpu.VMEM((sets, users * CLUSTERS, 2 * LANES), F32),
            pltpu.VMEM((sets, users * CLUSTERS, 2 * LANES), F32),
            dma((chips,)), dma((chips,)), dma((chips,)), dma((chips,)),
            dma((sets,)), dma((sets,)), dma((n,)), dma((n,)), dma((sets,)), dma((sets,)),
        ],
        compiler_params=pltpu.CompilerParams(
            collective_id=0, has_side_effects=True, vmem_limit_bytes=48 * 2**20
        ),
        name="zones",
    )(ray_rows, visible, base_tap, frac_index, elem_tap, elem_gain)

    block = 256
    return pl.pallas_call(
        element_kernel,
        grid=(elements // block,),
        out_shape=jax.ShapeDtypeStruct((users, elements, SAMPLES), F32),
        in_specs=[
            pl.BlockSpec((users * CLUSTERS, 2 * LANES), lambda step: (0, 0)),
            pl.BlockSpec((2 * CLUSTERS, block), lambda step: (0, step)),
        ],
        out_specs=pl.BlockSpec((users, block, SAMPLES), lambda step: (0, step, 0)),
        scratch_shapes=[pltpu.VMEM((3 * TAP_SPAN * CLUSTERS, users * LANES), BF16)],
        compiler_params=pltpu.CompilerParams(vmem_limit_bytes=48 * 2**20),
        name="elements",
    )(zones, elem)


def solution(mesh):
    in_specs = (
        P(("group", "link"), None),
        P(("group", "link"), None),
        P(("group", "link"), None),
        P(("group", "link"), None),
        P(None, "link"),
        P(None, "link"),
    )
    out_specs = P(("group", "link"), None, None)
    return jax.shard_map(
        functools.partial(on_device, mesh.shape["link"]),
        mesh=mesh, in_specs=in_specs, out_specs=out_specs, check_vma=False,
    )
```

time: 162 us -> 57.2 us (0.35)
  blocking collectives: 91.3 us -> 0 us
  Pallas kernels: 0 us -> 52.2 us
  local copies, waits for them, and re-layouts: 40 us -> 4.41 us
  matrix products: 14.5 us -> 0 us
  other arithmetic: 11.5 us -> 0 us
  starting transfers between devices: 3.86 us -> 0 us
    all_gather x2 -> x0, blocking collectives: 77.6 us -> none  [the longest x1 50.6 us: on_device(): lax.all_gather(elem_tap, 'link', axis=1, tiled=True)]
    pallas_call x0 -> x2, Pallas kernels: none -> 52.2 us  [the longest x1 44.6 us: on_device(): pl.pallas_call(functools.partial(zone_kernel, n, sets), out_shape=(jax.Sh...]
    gather x2 -> x0, local copies, waits for them, and re-layouts: 19.7 us -> none  [the longest x1 14.2 us: on_device(): ray_rows[lax.all_to_all(requests, 'link', split_axis=0, concat_axis=0, ti...]
    all_to_all x1 -> x0, blocking collectives: 13.7 us -> none  [on_device(): lax.all_to_all(requests, 'link', split_axis=0, concat_axis=0, tiled=True)]
    reshape x3 -> x0, local copies, waits for them, and re-layouts: 12.9 us -> none  [the longest x1 8.19 us: skew_sum(): sheared = flat.reshape(lead + (span, total_len - 1))]
    dot_general x2 -> x0, matrix products: 10.6 us -> none  [the longest x1 9.35 us: element_sum(): jnp.einsum('ucdn,cde->uen', windows, table, precision=lax.Precision.HIGHEST)]
    another operation x2 -> x0, other arithmetic: 4.71 us -> none
    unnamed x1 -> x0, matrix products: 3.89 us -> none
  transfers between devices with their start and end apart: 1 -> 0, of which waited for: 0 -> 0; matrix products, arithmetic and copies ran while one was open for 0% -> 0% of each run, Pallas kernels for 0% -> 0%
where the time goes in v1:
time: 57.2 us; the launch traced here: 56.6 us
  Pallas kernels  52.2 us (91%)
  local copies, waits for them, and re-layouts  4.41 us (8%)
    pallas_call x1, Pallas kernels, on_device(): pl.pallas_call(functools.partial(zone_kernel, n, sets), out_shape=(jax.Sh...  44.6 us
    pallas_call x1, Pallas kernels, on_device(): pl.pallas_call(element_kernel, grid=(elements // block,), out_shape=jax.S...  7.55 us
    unnamed x12, local copies, waits for them, and re-layouts  4.41 us

profile of v1, /device:TPU:0, one launch (start us, length us, event | category | flops | bytes accessed | tf_op | source)
XLA Modules:
  0.0 56.6 jit_solution(11901666790541177619)
XLA Ops:
  0.0 0.0 copy-start
  0.0 0.9 %copy-done = f32[512,128]{1,0:T(8,128)S(1)} copy-done((f32[512,128]{1,0:T(8,128)S(1)}, f32[512,128]{1,0:T(8,128)}, u32[]{:S(2)}) %copy-start) | copy-done | bytes 262168
  1.0 0.0 copy-start.1
  1.0 0.7 %copy-done.1 = s32[8,256]{1,0:T(8,128)S(1)} copy-done((s32[8,256]{1,0:T(8,128)S(1)}, s32[8,256]{1,0:T(8,128)}, u32[]{:S(2)}) %copy-start.1) | copy-done | bytes 8216
  1.6 0.0 copy-start.2
  1.7 0.7 %copy-done.2 = s32[8,256]{1,0:T(8,128)S(1)} copy-done((s32[8,256]{1,0:T(8,128)S(1)}, s32[8,256]{1,0:T(8,128)}, u32[]{:S(2)}) %copy-start.2) | copy-done | bytes 8216
  2.3 0.0 copy-start.3
  2.3 0.7 %copy-done.3 = s32[8,256]{1,0:T(8,128)S(1)} copy-done((s32[8,256]{1,0:T(8,128)S(1)}, s32[8,256]{1,0:T(8,128)}, u32[]{:S(2)}) %copy-start.3) | copy-done | bytes 8216
  3.0 0.0 copy-start.4
  3.0 0.7 %copy-done.4 = s32[8,128]{1,0:T(8,128)S(1)} copy-done((s32[8,128]{1,0:T(8,128)S(1)}, s32[8,128]{1,0:T(8,128)}, u32[]{:S(2)}) %copy-start.4) | copy-done | bytes 4120
  3.7 0.0 copy-start.5
  3.7 0.7 %copy-done.5 = f32[8,128]{1,0:T(8,128)S(1)} copy-done((f32[8,128]{1,0:T(8,128)S(1)}, f32[8,128]{1,0:T(8,128)}, u32[]{:S(2)}) %copy-start.5) | copy-done | bytes 4120
  4.4 44.6 %zones.1 = (f32[64,256]{1,0:T(8,128)S(1)}, f32[16,2048]{1,0:T(8,128)S(1)}) custom-call(f32[512,128]{1,0:T(8,128)S(1)} %copy-done, s32[8,256]{1,0:T(8,128)S(1)} %copy-done.1, s32[8,256]{1,0:T(8,128)S(1)} %copy-done.2, s32[8,256]{1,0:T(8,128)S(1)} %copy-done.3, s32[8,128]{1,0:T(8,128)S(1)} %copy-done.4, f32[8,128]{1,0:T(8,128)S(1)} %copy-done.5), custom_call_target="tpu_custom_call" | custom-call | tf_op jit(solution)/shard_map/zones/pallas_call | solution.py:272
  49.0 7.5 %elements.1 = f32[8,2048,128]{2,1,0:T(8,128)} custom-call(f32[64,256]{1,0:T(8,128)S(1)} %get-tuple-element.7.zone_ref, f32[16,2048]{1,0:T(8,128)S(1)} %get-tuple-element.8.elem_ref), custom_call_target="tpu_custom_call" | custom-call | tf_op jit(solution)/shard_map/elements/pallas_call | solution.py:300
Async XLA Ops:
  0.0 0.9 %copy-start = (f32[512,128]{1,0:T(8,128)S(1)}, f32[512,128]{1,0:T(8,128)}, u32[]{:S(2)}) copy-start(f32[512,128]{1,0:T(8,128)} %ray_ref.1) | copy-start | bytes 786436
  1.0 0.7 %copy-start.1 = (s32[8,256]{1,0:T(8,128)S(1)}, s32[8,256]{1,0:T(8,128)}, u32[]{:S(2)}) copy-start(s32[8,256]{1,0:T(8,128)} %vis_ref.1) | copy-start | bytes 24580
  1.6 0.7 %copy-start.2 = (s32[8,256]{1,0:T(8,128)S(1)}, s32[8,256]{1,0:T(8,128)}, u32[]{:S(2)}) copy-start(s32[8,256]{1,0:T(8,128)} %base_ref.1) | copy-start | bytes 24580
  2.3 0.7 %copy-start.3 = (s32[8,256]{1,0:T(8,128)S(1)}, s32[8,256]{1,0:T(8,128)}, u32[]{:S(2)}) copy-start(s32[8,256]{1,0:T(8,128)} %frac_ref.1) | copy-start | bytes 24580
  3.0 0.7 %copy-start.4 = (s32[8,128]{1,0:T(8,128)S(1)}, s32[8,128]{1,0:T(8,128)}, u32[]{:S(2)}) copy-start(s32[8,128]{1,0:T(8,128)} %tap_ref.1) | copy-start | bytes 12292
  3.7 0.7 %copy-start.5 = (f32[8,128]{1,0:T(8,128)S(1)}, f32[8,128]{1,0:T(8,128)}, u32[]{:S(2)}) copy-start(f32[8,128]{1,0:T(8,128)} %gain_ref.1) | copy-start | bytes 12292

commit v2 on v1

v2 whole, which is shorter than its diff:
```python
import functools

import jax
import jax.numpy as jnp
from jax import lax
from jax.experimental import pallas as pl
from jax.experimental.pallas import tpu as pltpu
from jax.sharding import PartitionSpec as P

SAMPLES = 128
TAP_SPAN = 32
BASE_SPAN = 64
FRACS = 16
CLUSTERS = 8
LANES = 128
TAPS = 4
PLACE_ROWS = -(-(BASE_SPAN + TAPS - 1) * CLUSTERS // 16) * 16
PICK_ROWS = 1024
PACK = 128 // TAP_SPAN
SETS = 2

F32 = jnp.float32
BF16 = jnp.bfloat16


def flip(value, mask, limit):
    result = value
    bit = 1
    while bit < limit:
        result = result + bit * ((mask // bit) % 2) * (1 - 2 * ((value // bit) % 2))
        bit *= 2
    return result


def split(value):
    high = value.astype(BF16)
    return high, (value - high.astype(F32)).astype(BF16)


def zone_kernel(
    n, sets,
    ray_ref, vis_hbm, base_hbm, frac_hbm, tap_hbm, gain_hbm,
    zone_ref, table_ref,
    vis_ref, base_ref, frac_ref, tap_ref, gain_ref,
    rays, elem_all, meta_own, meta_all, id_cols, ray_split, picked, places, table, zone_part,
    zone_got, load_sem, table_sem, ray_send, ray_recv, fwd_send, fwd_recv, meta_send, meta_recv, elem_send, elem_recv,
    zone_send, zone_recv,
):
    per_set = n // sets
    chips = per_set // 2
    me = lax.axis_index("link")
    own_set = me // per_set
    place = me % per_set
    chip = place // 2
    core = place % 2
    sibling = me + 1 - 2 * core
    users, slots = vis_ref.shape
    owned = ray_ref.shape[0]
    per_dev = tap_ref.shape[1]

    loads = [
        pltpu.make_async_copy(src, dst, load_sem.at[i])
        for i, (src, dst) in enumerate((
            (vis_hbm, vis_ref), (base_hbm, base_ref), (frac_hbm, frac_ref),
            (tap_hbm, tap_ref), (gain_hbm, gain_ref), (ray_ref, rays.at[0]),
        ))
    ]
    for load in loads:
        load.start()
    barrier = pltpu.get_barrier_semaphore()
    for step in range(1, n):
        pl.semaphore_signal(
            barrier, inc=1, device_id={"link": (me + step) % n}, device_id_type=pl.DeviceIdType.MESH
        )
    for load in loads[:-1]:
        load.wait()
    words = vis_ref[...] * (BASE_SPAN * FRACS) + base_ref[...] * FRACS + frac_ref[...]
    for part in range(slots // LANES):
        meta_own[part] = words[:, part * LANES : (part + 1) * LANES]
    meta_all[0] = meta_own[...]
    elem_all[me, 0:CLUSTERS] = gain_ref[...]
    elem_all[me, CLUSTERS : 2 * CLUSTERS] = (tap_ref[...] & (TAP_SPAN - 1)).astype(F32)
    picked[...] = jnp.zeros_like(picked)
    pl.semaphore_wait(barrier, n - 1)

    def remote(src, dst, send, recv, target):
        return pltpu.make_async_remote_copy(
            src_ref=src, dst_ref=dst, send_sem=send, recv_sem=recv,
            device_id={"link": target}, device_id_type=pl.DeviceIdType.MESH,
        )

    metas = [
        remote(meta_own, meta_all.at[q], meta_send.at[q], meta_recv.at[q],
               flip(own_set, q, sets) * per_set + place)
        for q in range(1, sets)
    ]
    for copy in metas:
        copy.start()
    elems = [
        remote(elem_all.at[me], elem_all.at[me], elem_send.at[step], elem_recv.at[step],
               (me + step) % n)
        for step in range(1, n)
    ]
    for copy in elems:
        copy.start()

    own_copy = remote(ray_ref, rays.at[1], fwd_send.at[0], fwd_recv.at[0], sibling)
    own_copy.start()

    def far_copy(k):
        return remote(ray_ref, rays.at[2 * k], ray_send.at[k], ray_recv.at[k],
                      own_set * per_set + flip(chip, k, chips) * 2 + core)

    def forward_copy(k):
        return remote(rays.at[2 * k], rays.at[2 * k + 1], fwd_send.at[k], fwd_recv.at[k], sibling)

    far = [far_copy(k) for k in range(1, chips)]
    for copy in far:
        copy.start()
    def expand():
        def body(index, carry):
            q, user = index // users, index % users
            for part in range(slots // LANES):
                row = meta_all[q, part, pl.ds(user, 1), :]
                ids = lax.shift_right_logical(row, jnp.int32(10))
                square = jnp.transpose(jnp.broadcast_to(ids, (LANES, LANES)))
                at = pl.multiple_of(index * slots + part * LANES, LANES)
                id_cols[pl.ds(at, LANES), :] = square
            return carry

        lax.fori_loop(0, sets * users, body, 0)

    def prepare(k):
        for other in range(2):
            high, low = split(rays[2 * k + other])
            ray_split[other * owned : (other + 1) * owned, 0:LANES] = high
            ray_split[other * owned : (other + 1) * owned, LANES : 2 * LANES] = low

    def pick(k):
        first = own_set * per_set + flip(chip, k, chips) * 2
        bases = ((first + core) * owned, (first + 1 - core) * owned)

        def body(chunk, carry):
            at = pl.multiple_of(chunk * PICK_ROWS, PICK_ROWS)
            ids = id_cols[pl.ds(at, PICK_ROWS), :]
            lane = lax.broadcasted_iota(jnp.int32, (PICK_ROWS, LANES), 1)
            hot = []
            for start in bases:
                shifted = ids - (lane + start)
                for tile in range(owned // LANES):
                    hot.append(jnp.where(shifted == tile * LANES, F32(1), F32(0)).astype(BF16))
            found = jnp.dot(
                jnp.concatenate(hot, axis=1), ray_split[...], preferred_element_type=F32
            )
            picked[pl.ds(at, PICK_ROWS), :] += found
            return carry

        lax.fori_loop(0, sets * users * slots // PICK_ROWS, body, 0)

    def weigh():
        def body(index, carry):
            q, user = index // users, index % users
            row = jnp.concatenate(
                [meta_all[q, part, pl.ds(user, 1), :] for part in range(slots // LANES)], axis=1
            )
            frac = (row & (FRACS - 1)).astype(F32) * F32(1.0 / FRACS)
            base = lax.shift_right_logical(row, jnp.int32(4)) & (BASE_SPAN - 1)
            cluster = lax.shift_right_logical(row, jnp.int32(10)) & (CLUSTERS - 1)
            weights = (
                -frac * (frac - 1.0) * (frac - 2.0) / 6.0,
                (frac + 1.0) * (frac - 1.0) * (frac - 2.0) / 2.0,
                -(frac + 1.0) * frac * (frac - 2.0) / 2.0,
                (frac + 1.0) * frac * (frac - 1.0) / 6.0,
            )
            offset = lax.broadcasted_iota(jnp.int32, (PLACE_ROWS, slots), 0) - (
                base * CLUSTERS + cluster
            )
            matrix = jnp.zeros((PLACE_ROWS, slots), F32)
            for tap in range(TAPS):
                matrix = jnp.where(offset == tap * CLUSTERS, weights[tap], matrix)
            high, low = split(matrix)
            places[index, 0] = high
            places[index, 1] = low
            return carry

        lax.fori_loop(0, sets * users, body, 0)

    def tabulate():
        owners = LANES // per_dev

        def body(tile, carry):
            both = jnp.concatenate(
                [elem_all[tile * owners + inner] for inner in range(owners)], axis=1
            )
            gain = both[0:CLUSTERS]
            tap = both[CLUSTERS : 2 * CLUSTERS]
            wide = jnp.concatenate(
                [jnp.where(tap == F32(delay), gain, F32(0)) for delay in range(TAP_SPAN)], axis=0
            )
            high, low = split(jnp.transpose(wide))
            at = pl.multiple_of(tile * LANES, LANES)
            depth = TAP_SPAN * CLUSTERS
            table[pl.ds(at, LANES), 0:depth] = high
            table[pl.ds(at, LANES), depth : 2 * depth] = low
            return carry

        lax.fori_loop(0, n // owners, body, 0)

    for copy in metas:
        copy.wait()
    expand()
    loads[-1].wait()
    own_copy.wait()
    store = pltpu.make_async_copy(table, table_ref, table_sem)

    def take(k, carry):
        @pl.when(k > 0)
        def _():
            far_copy(k).wait_recv()
            forward = forward_copy(k)
            forward.start()
            forward.wait_recv()

        prepare(k)
        pick(k)

        @pl.when(k == 0)
        def _():
            weigh()

        @pl.when(k == max(chips - 2, 0))
        def _():
            for copy in elems:
                copy.wait_recv()
            tabulate()
            store.start()

        return carry

    lax.fori_loop(0, chips, take, 0)

    def zones_of(q, pack):
        lane = lax.broadcasted_iota(jnp.int32, (CLUSTERS, LANES), 1)
        shared = jnp.zeros((CLUSTERS, LANES), F32)
        for inner in range(PACK):
            index = q * users + pack * PACK + inner
            rows = picked[pl.ds(pl.multiple_of(index * slots, slots), slots), :].astype(BF16)
            main = jnp.dot(places[index, 0], rows, preferred_element_type=F32)
            rest = jnp.dot(places[index, 1], rows[:, 0:LANES], preferred_element_type=F32)
            stacked = main[:, 0:LANES] + main[:, LANES : 2 * LANES] + rest
            early = stacked[0:CLUSTERS]
            late = jnp.zeros((CLUSTERS, LANES), F32)
            for delay in range(1, BASE_SPAN + TAPS - 1):
                turned = pltpu.roll(
                    stacked[delay * CLUSTERS : (delay + 1) * CLUSTERS], delay, axis=1
                )
                early = early + jnp.where(lane >= delay, turned, F32(0))
                late = late + jnp.where(lane < delay, turned, F32(0))
            zone_part[q, pack, inner * CLUSTERS : (inner + 1) * CLUSTERS, :] = early
            mine = late if inner == 0 else pltpu.roll(late, inner * TAP_SPAN, axis=1)
            inside = (lane >= inner * TAP_SPAN) & (lane < (inner + 1) * TAP_SPAN)
            shared = jnp.where(inside, mine, shared)
        zone_part[q, pack, PACK * CLUSTERS : (PACK + 1) * CLUSTERS, :] = shared

    packs = users // PACK

    def zone_copy(q, pack):
        return remote(zone_part.at[q, pack], zone_got.at[q, pack], zone_send.at[q, pack],
                      zone_recv.at[q, pack], flip(own_set, q, sets) * per_set + place)

    def make(index, carry):
        q, pack = sets - 1 - index // packs, index % packs
        zones_of(q, pack)

        @pl.when(q > 0)
        def _():
            zone_copy(q, pack).start()

        return carry

    lax.fori_loop(0, sets * packs, make, 0)
    for q in range(1, sets):
        for pack in range(packs):
            zone_copy(q, pack).wait()
    total = zone_part[0]
    for q in range(1, sets):
        total = total + zone_got[q]
    zone_ref[...] = total
    store.wait()
    for copy in elems:
        copy.wait_send()
    for k in range(1, chips):
        far_copy(k).wait_send()
        forward_copy(k).wait_send()


def element_kernel(zone_ref, table_ref, out_ref, windows):
    users = zone_ref.shape[0] * PACK
    depth = TAP_SPAN * CLUSTERS

    @pl.when(pl.program_id(0) == 0)
    def _():
        lane = lax.broadcasted_iota(jnp.int32, (CLUSTERS, LANES), 1)
        for user in range(users):
            pack, inner = user // PACK, user % PACK
            early = zone_ref[pack, inner * CLUSTERS : (inner + 1) * CLUSTERS, :]
            late = zone_ref[pack, PACK * CLUSTERS : (PACK + 1) * CLUSTERS, :]
            if inner:
                late = pltpu.roll(late, LANES - inner * TAP_SPAN, axis=1)
            tiles = []
            for delay in range(TAP_SPAN):
                ahead = TAP_SPAN - delay
                tiles.append(pltpu.roll(jnp.where(lane >= ahead, early, late), LANES - ahead, axis=1))
            high, low = split(jnp.concatenate(tiles, axis=0))
            at = user * LANES
            windows[0:depth, at : at + LANES] = high
            windows[depth : 2 * depth, at : at + LANES] = high
            windows[2 * depth : 3 * depth, at : at + LANES] = low

    both = table_ref[...]
    result = jnp.dot(
        jnp.concatenate([both, both[:, 0:depth]], axis=1), windows[...], preferred_element_type=F32
    )
    for user in range(users):
        out_ref[user] = result[:, user * LANES : (user + 1) * LANES]


def on_device(n, ray_rows, visible, base_tap, frac_index, elem_tap, elem_gain):
    users, slots = visible.shape
    owned = ray_rows.shape[0]
    per_dev = elem_tap.shape[1]
    elements = n * per_dev
    sets = SETS
    per_set = n // sets
    chips = per_set // 2
    dma = pltpu.SemaphoreType.DMA
    vmem = pl.BlockSpec(memory_space=pltpu.VMEM)
    hbm = pl.BlockSpec(memory_space=pl.ANY)
    packs = users // PACK
    depth = TAP_SPAN * CLUSTERS
    packed = ((PACK + 1) * CLUSTERS, LANES)
    zones, table = pl.pallas_call(
        functools.partial(zone_kernel, n, sets),
        out_shape=(
            jax.ShapeDtypeStruct((packs,) + packed, F32),
            jax.ShapeDtypeStruct((elements, 2 * depth), BF16),
        ),
        in_specs=[hbm] * 6,
        out_specs=(vmem, hbm),
        scratch_shapes=[
            pltpu.VMEM((users, slots), jnp.int32),
            pltpu.VMEM((users, slots), jnp.int32),
            pltpu.VMEM((users, slots), jnp.int32),
            pltpu.VMEM((CLUSTERS, per_dev), jnp.int32),
            pltpu.VMEM((CLUSTERS, per_dev), F32),
            pltpu.VMEM((per_set, owned, LANES), F32),
            pltpu.VMEM((n, 2 * CLUSTERS, per_dev), F32),
            pltpu.VMEM((slots // LANES, users, LANES), jnp.int32),
            pltpu.VMEM((sets, slots // LANES, users, LANES), jnp.int32),
            pltpu.VMEM((sets * users * slots, LANES), jnp.int32),
            pltpu.VMEM((2 * owned, 2 * LANES), BF16),
            pltpu.VMEM((sets * users * slots, 2 * LANES), F32),
            pltpu.VMEM((sets * users, 2, PLACE_ROWS, slots), BF16),
            pltpu.VMEM((elements, 2 * depth), BF16),
            pltpu.VMEM((sets, packs) + packed, F32),
            pltpu.VMEM((sets, packs) + packed, F32),
            dma((6,)), dma,
            dma((chips,)), dma((chips,)), dma((chips,)), dma((chips,)),
            dma((sets,)), dma((sets,)), dma((n,)), dma((n,)),
            dma((sets, packs)), dma((sets, packs)),
        ],
        compiler_params=pltpu.CompilerParams(
            collective_id=0, has_side_effects=True, vmem_limit_bytes=56 * 2**20
        ),
        name="zones",
    )(ray_rows, visible, base_tap, frac_index, elem_tap, elem_gain)

    block = 512
    return pl.pallas_call(
        element_kernel,
        grid=(elements // block,),
        out_shape=jax.ShapeDtypeStruct((users, elements, SAMPLES), F32),
        in_specs=[
            pl.BlockSpec((packs,) + packed, lambda step: (0, 0, 0)),
            pl.BlockSpec((block, 2 * depth), lambda step: (step, 0)),
        ],
        out_specs=pl.BlockSpec((users, block, SAMPLES), lambda step: (0, step, 0)),
        scratch_shapes=[pltpu.VMEM((3 * depth, users * LANES), BF16)],
        compiler_params=pltpu.CompilerParams(vmem_limit_bytes=63 * 2**20),
        name="elements",
    )(zones, table)


def solution(mesh):
    in_specs = (
        P(("group", "link"), None),
        P(("group", "link"), None),
        P(("group", "link"), None),
        P(("group", "link"), None),
        P(None, "link"),
        P(None, "link"),
    )
    out_specs = P(("group", "link"), None, None)
    return jax.shard_map(
        functools.partial(on_device, mesh.shape["link"]),
        mesh=mesh, in_specs=in_specs, out_specs=out_specs, check_vma=False,
    )
```

time: 57.2 us -> 46 us (0.80)
  Pallas kernels: 52.2 us -> 45.7 us
  local copies, waits for them, and re-layouts: 4.41 us -> 0 us
    pallas_call x1, Pallas kernels: 44.6 us -> 37.9 us  [on_device(): pl.pallas_call(functools.partial(zone_kernel, n, sets), out_shape=(jax.Sh...]
    unnamed x12 -> x0, local copies, waits for them, and re-layouts: 4.41 us -> none
where the time goes in v2:
time: 46 us; the launch traced here: 45.8 us
  Pallas kernels  45.7 us (99%)
    pallas_call x1, Pallas kernels, on_device(): pl.pallas_call(functools.partial(zone_kernel, n, sets), out_shape=(jax.Sh...  37.9 us
    pallas_call x1, Pallas kernels, on_device(): pl.pallas_call(element_kernel, grid=(elements // block,), out_shape=jax.S...  7.87 us

profile of v2, /device:TPU:0, one launch (start us, length us, event | category | flops | bytes accessed | tf_op | source)
XLA Modules:
  0.0 45.8 jit_solution(13866727098854565747)
XLA Ops:
  0.0 37.9 %zones.1 = (f32[2,40,128]{2,1,0:T(8,128)}, bf16[2048,512]{1,0:T(8,128)(2,1)}) custom-call(f32[512,128]{1,0:T(8,128)} %ray_ref.1, s32[8,256]{1,0:T(8,128)} %vis_hbm.1, s32[8,256]{1,0:T(8,128)} %base_hbm.1, s32[8,256]{1,0:T(8,128)} %frac_hbm.1, s32[8,128]{1,0:T(8,128)} %tap_hbm.1, f32[8,128]{1,0:T(8,128)} %gain_hbm.1), custom_call_target="tpu_custom_call" | custom-call | tf_op jit(solution)/shard_map/zones/pallas_call | solution.py:342
  37.9 7.9 %elements.1 = f32[8,2048,128]{2,1,0:T(8,128)} custom-call(f32[2,40,128]{2,1,0:T(8,128)} %get-tuple-element.7.zone_ref, bf16[2048,512]{1,0:T(8,128)(2,1)} %get-tuple-element.8.table_ref), custom_call_target="tpu_custom_call" | custom-call | tf_op jit(solution)/shard_map/elements/pallas_call | solution.py:379

commit v3 on v2

--- a/solution.py
+++ b/solution.py
@@ -15,7 +15,7 @@
 LANES = 128
 TAPS = 4
 PLACE_ROWS = -(-(BASE_SPAN + TAPS - 1) * CLUSTERS // 16) * 16
-PICK_ROWS = 1024
+PICK_ROWS = 2048
 PACK = 128 // TAP_SPAN
 SETS = 2
 
@@ -80,7 +80,56 @@
     meta_all[0] = meta_own[...]
     elem_all[me, 0:CLUSTERS] = gain_ref[...]
     elem_all[me, CLUSTERS : 2 * CLUSTERS] = (tap_ref[...] & (TAP_SPAN - 1)).astype(F32)
+    def expand(first, last):
+        def body(index, carry):
+            q, user = index // users, index % users
+            for part in range(slots // LANES):
+                row = meta_all[q, part, pl.ds(user, 1), :]
+                ids = lax.shift_right_logical(row, jnp.int32(10))
+                square = jnp.transpose(jnp.broadcast_to(ids, (LANES, LANES)))
+                at = pl.multiple_of(index * slots + part * LANES, LANES)
+                id_cols[pl.ds(at, LANES), :] = square
+            return carry
+
+        lax.fori_loop(first, last, body, 0)
+
+    def weigh(first, last):
+        def body(index, carry):
+            q, user = index // users, index % users
+            row = jnp.concatenate(
+                [meta_all[q, part, pl.ds(user, 1), :] for part in range(slots // LANES)], axis=1
+            )
+            frac = (row & (FRACS - 1)).astype(F32) * F32(1.0 / FRACS)
+            base = lax.shift_right_logical(row, jnp.int32(4)) & (BASE_SPAN - 1)
+            cluster = lax.shift_right_logical(row, jnp.int32(10)) & (CLUSTERS - 1)
+            weights = (
+                -frac * (frac - 1.0) * (frac - 2.0) / 6.0,
+                (frac + 1.0) * (frac - 1.0) * (frac - 2.0) / 2.0,
+                -(frac + 1.0) * frac * (frac - 2.0) / 2.0,
+                (frac + 1.0) * frac * (frac - 1.0) / 6.0,
+            )
+            delays = PLACE_ROWS // CLUSTERS
+            offset = lax.broadcasted_iota(jnp.int32, (delays, slots), 0) - base
+            matrix = jnp.zeros((delays, slots), F32)
+            for tap in range(TAPS):
+                matrix = jnp.where(offset == tap, weights[tap], matrix)
+            top = matrix.astype(BF16).astype(F32)
+            member = lax.broadcasted_iota(jnp.int32, (CLUSTERS, slots), 0) == cluster
+
+            def by_cluster(values):
+                return jnp.concatenate(
+                    [jnp.where(member, values[at : at + 1], F32(0)) for at in range(delays)], axis=0
+                ).astype(BF16)
+
+            high, low = by_cluster(top), by_cluster(matrix - top)
+            places[index, 0] = high
+            places[index, 1] = low
+            return carry
+
+        lax.fori_loop(first, last, body, 0)
+
     picked[...] = jnp.zeros_like(picked)
+    expand(0, users)
     pl.semaphore_wait(barrier, n - 1)
 
     def remote(src, dst, send, recv, target):
@@ -117,19 +166,6 @@
     far = [far_copy(k) for k in range(1, chips)]
     for copy in far:
         copy.start()
-    def expand():
-        def body(index, carry):
-            q, user = index // users, index % users
-            for part in range(slots // LANES):
-                row = meta_all[q, part, pl.ds(user, 1), :]
-                ids = lax.shift_right_logical(row, jnp.int32(10))
-                square = jnp.transpose(jnp.broadcast_to(ids, (LANES, LANES)))
-                at = pl.multiple_of(index * slots + part * LANES, LANES)
-                id_cols[pl.ds(at, LANES), :] = square
-            return carry
-
-        lax.fori_loop(0, sets * users, body, 0)
-
     def prepare(k):
         for other in range(2):
             high, low = split(rays[2 * k + other])
@@ -156,34 +192,6 @@
             return carry
 
         lax.fori_loop(0, sets * users * slots // PICK_ROWS, body, 0)
-
-    def weigh():
-        def body(index, carry):
-            q, user = index // users, index % users
-            row = jnp.concatenate(
-                [meta_all[q, part, pl.ds(user, 1), :] for part in range(slots // LANES)], axis=1
-            )
-            frac = (row & (FRACS - 1)).astype(F32) * F32(1.0 / FRACS)
-            base = lax.shift_right_logical(row, jnp.int32(4)) & (BASE_SPAN - 1)
-            cluster = lax.shift_right_logical(row, jnp.int32(10)) & (CLUSTERS - 1)
-            weights = (
-                -frac * (frac - 1.0) * (frac - 2.0) / 6.0,
-                (frac + 1.0) * (frac - 1.0) * (frac - 2.0) / 2.0,
-                -(frac + 1.0) * frac * (frac - 2.0) / 2.0,
-                (frac + 1.0) * frac * (frac - 1.0) / 6.0,
-            )
-            offset = lax.broadcasted_iota(jnp.int32, (PLACE_ROWS, slots), 0) - (
-                base * CLUSTERS + cluster
-            )
-            matrix = jnp.zeros((PLACE_ROWS, slots), F32)
-            for tap in range(TAPS):
-                matrix = jnp.where(offset == tap * CLUSTERS, weights[tap], matrix)
-            high, low = split(matrix)
-            places[index, 0] = high
-            places[index, 1] = low
-            return carry
-
-        lax.fori_loop(0, sets * users, body, 0)
 
     def tabulate():
         owners = LANES // per_dev
@@ -206,9 +214,10 @@
 
         lax.fori_loop(0, n // owners, body, 0)
 
+    weigh(0, users)
     for copy in metas:
         copy.wait()
-    expand()
+    expand(users, sets * users)
     loads[-1].wait()
     own_copy.wait()
     store = pltpu.make_async_copy(table, table_ref, table_sem)
@@ -226,7 +235,7 @@
 
         @pl.when(k == 0)
         def _():
-            weigh()
+            weigh(users, sets * users)
 
         @pl.when(k == max(chips - 2, 0))
         def _():
@@ -318,11 +327,12 @@
             windows[2 * depth : 3 * depth, at : at + LANES] = low
 
     both = table_ref[...]
-    result = jnp.dot(
-        jnp.concatenate([both, both[:, 0:depth]], axis=1), windows[...], preferred_element_type=F32
-    )
-    for user in range(users):
-        out_ref[user] = result[:, user * LANES : (user + 1) * LANES]
+    terms = jnp.concatenate([both, both[:, 0:depth]], axis=1)
+    for user in range(0, users, 2):
+        at = user * LANES
+        pair = jnp.dot(terms, windows[:, at : at + 2 * LANES], preferred_element_type=F32)
+        out_ref[user] = pair[:, 0:LANES]
+        out_ref[user + 1] = pair[:, LANES : 2 * LANES]
 
 
 def on_device(n, ray_rows, visible, base_tap, frac_index, elem_tap, elem_gain):
@@ -375,7 +385,7 @@
         name="zones",
     )(ray_rows, visible, base_tap, frac_index, elem_tap, elem_gain)
 
-    block = 512
+    block = 1024
     return pl.pallas_call(
         element_kernel,
         grid=(elements // block,),

time: 46 us -> 41.3 us (0.90)
  Pallas kernels: 45.7 us -> 41 us
    pallas_call x1, Pallas kernels: 37.9 us -> 33.4 us  [on_device(): pl.pallas_call(functools.partial(zone_kernel, n, sets), out_shape=(jax.Sh...]
where the time goes in v3:
time: 41.3 us; the launch traced here: 41.1 us
  Pallas kernels  41 us (99%)
    pallas_call x1, Pallas kernels, on_device(): pl.pallas_call(functools.partial(zone_kernel, n, sets), out_shape=(jax.Sh...  33.4 us
    pallas_call x1, Pallas kernels, on_device(): pl.pallas_call(element_kernel, grid=(elements // block,), out_shape=jax.S...  7.61 us

profile of v3, /device:TPU:0, one launch (start us, length us, event | category | flops | bytes accessed | tf_op | source)
XLA Modules:
  0.0 41.1 jit_solution(2961943155181308624)
XLA Ops:
  0.0 33.4 %zones.1 = (f32[2,40,128]{2,1,0:T(8,128)}, bf16[2048,512]{1,0:T(8,128)(2,1)}) custom-call(f32[512,128]{1,0:T(8,128)} %ray_ref.1, s32[8,256]{1,0:T(8,128)} %vis_hbm.1, s32[8,256]{1,0:T(8,128)} %base_hbm.1, s32[8,256]{1,0:T(8,128)} %frac_hbm.1, s32[8,128]{1,0:T(8,128)} %tap_hbm.1, f32[8,128]{1,0:T(8,128)} %gain_hbm.1), custom_call_target="tpu_custom_call" | custom-call | tf_op jit(solution)/shard_map/zones/pallas_call | solution.py:352
  33.4 7.6 %elements.1 = f32[8,2048,128]{2,1,0:T(8,128)} custom-call(f32[2,40,128]{2,1,0:T(8,128)} %get-tuple-element.7.zone_ref, bf16[2048,512]{1,0:T(8,128)(2,1)} %get-tuple-element.8.table_ref), custom_call_target="tpu_custom_call" | custom-call | tf_op jit(solution)/shard_map/elements/pallas_call | solution.py:389

commit v4 on v3

--- a/solution.py
+++ b/solution.py
@@ -15,7 +15,7 @@
 LANES = 128
 TAPS = 4
 PLACE_ROWS = -(-(BASE_SPAN + TAPS - 1) * CLUSTERS // 16) * 16
-PICK_ROWS = 2048
+PICK_ROWS = 4096
 PACK = 128 // TAP_SPAN
 SETS = 2
 

time: 41.3 us -> 40.4 us (0.978)
  Pallas kernels: 41 us -> 40.2 us
    pallas_call x1, Pallas kernels: 33.4 us -> 32.6 us  [on_device(): pl.pallas_call(functools.partial(zone_kernel, n, sets), out_shape=(jax.Sh...]
where the time goes in v4:
time: 40.4 us; the launch traced here: 40.2 us
  Pallas kernels  40.2 us (100%)
    pallas_call x1, Pallas kernels, on_device(): pl.pallas_call(functools.partial(zone_kernel, n, sets), out_shape=(jax.Sh...  32.6 us
    pallas_call x1, Pallas kernels, on_device(): pl.pallas_call(element_kernel, grid=(elements // block,), out_shape=jax.S...  7.61 us

profile of v4, /device:TPU:0, one launch (start us, length us, event | category | flops | bytes accessed | tf_op | source)
XLA Modules:
  0.0 40.2 jit_solution(856826832878797069)
XLA Ops:
  0.0 32.6 %zones.1 = (f32[2,40,128]{2,1,0:T(8,128)}, bf16[2048,512]{1,0:T(8,128)(2,1)}) custom-call(f32[512,128]{1,0:T(8,128)} %ray_ref.1, s32[8,256]{1,0:T(8,128)} %vis_hbm.1, s32[8,256]{1,0:T(8,128)} %base_hbm.1, s32[8,256]{1,0:T(8,128)} %frac_hbm.1, s32[8,128]{1,0:T(8,128)} %tap_hbm.1, f32[8,128]{1,0:T(8,128)} %gain_hbm.1), custom_call_target="tpu_custom_call" | custom-call | tf_op jit(solution)/shard_map/zones/pallas_call | solution.py:352
  32.6 7.6 %elements.1 = f32[8,2048,128]{2,1,0:T(8,128)} custom-call(f32[2,40,128]{2,1,0:T(8,128)} %get-tuple-element.7.zone_ref, bf16[2048,512]{1,0:T(8,128)(2,1)} %get-tuple-element.8.table_ref), custom_call_target="tpu_custom_call" | custom-call | tf_op jit(solution)/shard_map/elements/pallas_call | solution.py:389
